TPU v7x, 512 devices: a whole 4x8x8 slice. The times are simulated.
512 devices in a mesh: gy: 16 (over z_hi, y), gz: 4 (over z_lo), band: 8 (over x, core).
Axes of the slice: x: 4, y: 8, z: 8 (z_hi: 2, z_lo: 4; z = z_hi * 4 + z_lo), core: 2. Of those that a mesh axis runs over, the one named last changes fastest.
Arguments:
- previous: float32 [128, 128, 32, 128], P('band', 'gy', 'gz'), may hold values from -2.4 to 2.4
- current: float32 [128, 128, 32, 128], P('band', 'gy', 'gz'), may hold values from 0.5 to 4.5
- potential: float32 [128, 32, 128], P('gy', 'gz'), may hold values from 0 to 2
- projectors: float32 [64, 128, 32, 128], P(None, 'gy', 'gz'), may hold values from -0.0625 to 0.0625
- couplings: float32 [64], replicated, may hold values from 0.5 to 2
- pattern: int32 [8, 64], replicated, may hold values 0 or 1
- counts: int32 [8], replicated, may hold values from 1 to 8, as said below
- panels: float32 [256, 128, 32, 128], P('band', 'gy', 'gz'), may hold values from -0.03125 to 0.03125
Outputs:
- rotated: float32 [128, 128, 32, 128], P('band', 'gy', 'gz')
- coefficients: float32 [256, 128], P(None, 'band')
Inputs may be any that keep to these rules, and one draw needn't show every extreme that they name: `counts`: some atom block has all 8 slots live.
All inputs are finite; a program needn't handle non-finite values.
Results may differ from a plain program's by a relative error of at most 0.00011.
Values sent between devices are 32-bit elements; how exact they have to be, the bound alone decides.
A program may use at most 128 MiB of HBM per device.

v0:
```python
import jax
import jax.numpy as jnp
from jax import lax
from jax.sharding import PartitionSpec as P

STENCIL = (
    -5369.0 / 1800.0,
    12.0 / 7.0,
    -15.0 / 56.0,
    10.0 / 189.0,
    -1.0 / 112.0,
    2.0 / 1925.0,
    -1.0 / 16632.0,
)
CENTER = 1.0
HALF_WIDTH = 5.0


def extended_2(block, sides, width):
    for axis, dim in sides:
        count = lax.axis_size(axis)
        forward = [(i, i + 1) for i in range(count - 1)]
        forward.append((count - 1, 0))
        backward = [(target, source) for source, target in forward]
        low = lax.ppermute(
            lax.slice_in_dim(block, block.shape[dim] - width, None, axis=dim), axis, forward
        )
        high = lax.ppermute(lax.slice_in_dim(block, 0, width, axis=dim), axis, backward)
        block = jnp.concatenate([low, block, high], axis=dim)
    return block


def exact_dot(left, right):
    return jnp.dot(left, right, precision=lax.Precision.HIGHEST, preferred_element_type=jnp.float32)


def per_device(previous, current, potential, projectors, couplings, pattern, counts, panels):
    blocks, rows_y, rows_z, width_x = current.shape
    cell_count = rows_y * rows_z * width_x
    extended = extended_2(current, (("gy", 1), ("gz", 2)), 6)
    laplacian = 3.0 * STENCIL[0] * current
    for reach in range(1, 7):
        laplacian = laplacian + STENCIL[reach] * (
            jnp.roll(current, reach, 3)
            + jnp.roll(current, -reach, 3)
            + extended[:, 6 + reach : 6 + reach + rows_y, 6 : 6 + rows_z]
            + extended[:, 6 - reach : 6 - reach + rows_y, 6 : 6 + rows_z]
            + extended[:, 6 : 6 + rows_y, 6 + reach : 6 + reach + rows_z]
            + extended[:, 6 : 6 + rows_y, 6 - reach : 6 - reach + rows_z]
        )
    own_tile = lax.axis_index("gy") * lax.axis_size("gz") + lax.axis_index("gz")
    tile_count = pattern.shape[1]
    per_block = projectors.shape[0] // counts.shape[0]
    touched = jnp.sum(
        jnp.where(jnp.arange(tile_count)[None, :] == own_tile, pattern, 0), axis=1
    ).astype(jnp.float32)
    slot_live = (jnp.arange(per_block)[None, :] < counts[:, None]).astype(jnp.float32)
    weight = (touched[:, None] * slot_live).reshape(-1)
    flat_block = current.reshape(blocks, cell_count)
    proj_rows = projectors.reshape(projectors.shape[0], cell_count)
    partial_value = exact_dot(proj_rows, flat_block.T) * weight[:, None]
    base = (
        2.0 / HALF_WIDTH * (-0.5 * laplacian + potential * current - CENTER * current) - previous
    ).reshape(blocks, cell_count)
    own_rows = panels.reshape(panels.shape[0], cell_count)
    proj_sums = lax.psum(partial_value, ("gy", "gz"))
    projected = exact_dot(((couplings * weight)[:, None] * proj_sums).T, proj_rows)
    filtered = base + 2.0 / HALF_WIDTH * projected
    gathered = lax.all_gather(own_rows, "band", axis=0, tiled=True)
    intersection = exact_dot(gathered, filtered.T)
    coefficients = lax.psum(intersection, ("gy", "gz"))
    rotated = filtered - exact_dot(coefficients.T, gathered)
    return (rotated.reshape(blocks, rows_y, rows_z, width_x), coefficients)


def solution(mesh):
    in_specs = (
        P("band", "gy", "gz", None),
        P("band", "gy", "gz", None),
        P("gy", "gz", None),
        P(None, "gy", "gz", None),
        P(),
        P(),
        P(),
        P("band", "gy", "gz", None),
    )
    out_specs = (P("band", "gy", "gz", None), P(None, "band"))
    return jax.shard_map(
        per_device, mesh=mesh, in_specs=in_specs, out_specs=out_specs, check_vma=False
    )
```

profile of v0, /device:TPU:38, one launch (start us, length us, event | category | flops | bytes accessed | tf_op | source)
XLA Modules:
  0.0 708.4 jit_solution(8966925279136649046)
XLA Ops:
  7.2 2.9 copy.95
  10.3 2.6 collective-permute-start.1
  13.1 4.5 collective-permute-start
  17.7 0.2 fusion.67
  18.0 0.2 fusion.64
  18.2 0.2 fusion.65
  18.4 0.2 fusion.62
  18.6 0.2 fusion.63
  18.8 0.2 fusion.60
  19.0 0.2 fusion.61
  19.2 0.2 fusion.58
  19.5 0.2 fusion.59
  19.7 0.3 copy.71
  20.0 0.3 copy.72
  20.3 1.1 copy.73
  21.4 1.1 copy.74
  22.5 1.1 copy.75
  23.6 1.1 copy.76
  24.7 1.1 copy.77
  25.8 1.1 copy.78
  26.9 1.1 copy.79
  28.0 1.1 copy.80
  29.1 1.1 copy.81
  30.2 1.1 copy.82
  31.3 1.1 copy.83
  32.4 1.1 copy.84
  33.5 1.1 copy.85
  34.6 1.1 copy.86
  35.7 1.1 copy.87
  36.8 1.1 copy.88
  37.9 1.1 copy.89
  39.1 1.1 copy.90
  40.4 1.1 copy.91
  41.5 0.3 constant_dynamic-update-slice_fusion.1
  42.0 1.6 fusion.55
  43.6 7.9 %collective-permute-start.2 = (f32[16,20,6,128]{3,0,2,1:T(8,128)}, f32[16,20,6,128]{3,0,2,1:T(8,128)}, u32[]{:S(2)}, u32[]{:S(2)}) collective-permute-start(f32[16,20,6,128]{3,0,2,1:T(8,128)} %get-tuple-element.2), channel_id=1, source_target_pairs={{8,0},{16,8},{24,16},{0,24},{9,1},{17,9},{25,17},{1,25},{10,2},{18... | collective-permute-start | bytes 2949128 | tf_op jit(solution)/shard_map/ppermute | solution.py:28
  51.5 2.1 collective-permute-start.3
  53.9 1.1 copy.92
  55.0 1.2 copy.93
  56.1 1.2 copy.94
  57.6 4.7 fusion.9
  62.3 319.1 %psum.14 = f32[64,16]{1,0:T(8,128)S(1)} all-reduce(f32[64,16]{1,0:T(8,128)S(1)} %fusion.9), channel_id=1, replica_groups=mesh['gy'=16,'gz'=4,'band'=8] {'gy','gz'}, use_global_device_ids=true, to_apply=%region_1.2 | all-reduce | flops 1024 | bytes 8192 | tf_op jit(solution)/shard_map/psum | solution.py:66
  381.4 8.6 %fusion.21 = f32[16,8,8,128]{3,0,2,1:T(8,128)S(1)} fusion(f32[16,20,8,128]{3,0,2,1:T(8,128)} %copy-done.1, f32[16,20,6,128]{3,0,2,1:T(8,128)} %collective-permute-done.3, f32[16,20,6,128]{3,0,2,1:T(8,128)} %collective-permute-done.2, f32[16,14,8,128]{3,0,2,1:T(8,128)S(1)} %get-tuple-element.29, f32[16,14,8,128]{3,0,2,1:T(8,128)S(1)} %get-tuple-element.33, ...), kind=kLoop, calls=%fused_computation.41 | loop fusion | flops 9568256 | bytes 17465344 | tf_op jit(solution)/shard_map/sub | solution.py:63
  390.1 2.5 fusion
  392.6 8.9 %convolution_bitcast_fusion = f32[256,16]{0,1:T(8,128)S(1)} fusion(f32[16,8192]{1,0:T(8,128)S(1)} %fusion, f32[256,8192]{1,0:T(8,128)} %all-gather.2.cloned.1.call-done), kind=kOutput, calls=%fused_computation.30 | convolution fusion | flops 402653184 | bytes 8929280 | tf_op jit(solution)/shard_map/dot_general | solution.py:34
  401.5 292.8 %psum.15 = f32[256,16]{0,1:T(8,128)S(1)} all-reduce(f32[256,16]{0,1:T(8,128)S(1)} %convolution_bitcast_fusion), channel_id=1, replica_groups=mesh['gy'=16,'gz'=4,'band'=8] {'gy','gz'}, use_global_device_ids=true, to_apply=%region_2.3 | all-reduce | flops 4096 | bytes 32768 | tf_op jit(solution)/shard_map/psum | solution.py:71
  694.3 6.4 fusion.5
  700.7 0.9 copy.49
  (38 shorter events, 1.6 us)
Async XLA Ops:
  7.2 3.0 copy-start
  7.2 385.5 %all-gather.2.cloned.1.call-start = ((), (), s32[]{:S(2)}) async-start(), calls=%async_computation | async-start | bytes 9437184 | tf_op jit(solution)/shard_map/all_gather | solution.py:69
  10.3 31.1 %collective-permute-start.1 = (f32[16,6,8,128]{3,0,2,1:T(8,128)S(1)}, f32[16,6,8,128]{3,0,2,1:T(8,128)S(1)}, u32[]{:S(2)}, u32[]{:S(2)}) collective-permute-start(f32[16,6,8,128]{3,0,2,1:T(8,128)S(1)} %copy.69), channel_id=1, source_target_pairs={{0,32},{32,64},{64,96},{96,128},{128,160},{160,192},{192,224},{224... | collective-permute-start | bytes 1179656 | tf_op jit(solution)/shard_map/ppermute | solution.py:25
  13.1 28.8 %collective-permute-start = (f32[16,6,8,128]{3,0,2,1:T(8,128)S(1)}, f32[16,6,8,128]{3,0,2,1:T(8,128)S(1)}, u32[]{:S(2)}, u32[]{:S(2)}) collective-permute-start(f32[16,6,8,128]{3,0,2,1:T(8,128)S(1)} %copy.70), channel_id=1, source_target_pairs={{32,0},{64,32},{96,64},{128,96},{160,128},{192,160},{224,192},{256... | collective-permute-start | bytes 1179656 | tf_op jit(solution)/shard_map/ppermute | solution.py:28
  42.0 11.9 %copy-start.1 = (f32[16,20,8,128]{3,0,2,1:T(8,128)}, f32[16,20,8,128]{3,0,2,1:T(8,128)S(1)}, u32[]{:S(2)}) copy-start(f32[16,20,8,128]{3,0,2,1:T(8,128)S(1)} %get-tuple-element.34) | copy-start | bytes 3932164
  43.6 337.8 %collective-permute-start.2 = (f32[16,20,6,128]{3,0,2,1:T(8,128)}, f32[16,20,6,128]{3,0,2,1:T(8,128)}, u32[]{:S(2)}, u32[]{:S(2)}) collective-permute-start(f32[16,20,6,128]{3,0,2,1:T(8,128)} %get-tuple-element.2), channel_id=1, source_target_pairs={{8,0},{16,8},{24,16},{0,24},{9,1},{17,9},{25,17},{1,25},{10,2},{18... | collective-permute-start | bytes 2949128 | tf_op jit(solution)/shard_map/ppermute | solution.py:28
  51.5 329.9 %collective-permute-start.3 = (f32[16,20,6,128]{3,0,2,1:T(8,128)}, f32[16,20,6,128]{3,0,2,1:T(8,128)}, u32[]{:S(2)}, u32[]{:S(2)}) collective-permute-start(f32[16,20,6,128]{3,0,2,1:T(8,128)} %get-tuple-element.3), channel_id=1, source_target_pairs={{0,8},{8,16},{16,24},{24,0},{1,9},{9,17},{17,25},{25,1},{2,10},{10... | collective-permute-start | bytes 2949128 | tf_op jit(solution)/shard_map/ppermute | solution.py:25
  53.8 3.5 copy-start.5
  53.8 3.6 copy-start.6
  53.9 3.7 copy-start.7
  56.1 325.3 %copy-start.4 = (f32[8,8,128]{2,1,0:T(8,128)S(1)}, f32[8,8,128]{2,1,0:T(8,128)}, u32[]{:S(2)}) copy-start(f32[8,8,128]{2,1,0:T(8,128)} %param.10) | copy-start | bytes 98308
  381.4 8.8 %copy-start.2 = (f32[64,8,8,128]{3,2,1,0:T(8,128)S(1)}, f32[64,8,8,128]{3,2,1,0:T(8,128)}, u32[]{:S(2)}) copy-start(f32[64,8,8,128]{3,2,1,0:T(8,128)} %param.11) | copy-start | bytes 6291460
  694.3 6.4 copy-start.3
Sparse Core Ops, SparseCore 0:
  10.2 57.5 all-gather.1
where the time goes:
time: 709 us; the launch traced here: 708 us
  blocking collectives  612 us (86%)
  local copies, waits for them, and re-layouts  34 us (5%)
  matrix products  22.4 us (3%)
  starting transfers between devices  17.1 us (2%)
  between operations  14.3 us (2%)
  other arithmetic  8.76 us (1%)
    psum x1, blocking collectives, per_device(): proj_sums = lax.psum(partial_value, ('gy', 'gz'))  319 us
    psum x1, blocking collectives, per_device(): coefficients = lax.psum(intersection, ('gy', 'gz'))  293 us
    unnamed x46, local copies, waits for them, and re-layouts  29.4 us
    dot_general x4, matrix products, exact_dot(): jnp.dot(left, right, precision=lax.Precision.HIGHEST, preferred_element_t...  22.4 us
  transfers between devices with their start and end apart: 5, of which 0 were waited for; matrix products, arithmetic and copies ran while one was open for 7% of the time, Pallas kernels for 0%

commit v1 on v0

v1 whole, which is shorter than its diff:
```python
import jax
import jax.numpy as jnp
from jax import lax
from jax.experimental import pallas as pl
from jax.experimental.pallas import tpu as pltpu
from jax.sharding import PartitionSpec as P

STENCIL = (
    -5369.0 / 1800.0,
    12.0 / 7.0,
    -15.0 / 56.0,
    10.0 / 189.0,
    -1.0 / 112.0,
    2.0 / 1925.0,
    -1.0 / 16632.0,
)
CENTER = 1.0
HALF_WIDTH = 5.0
SCALE = 2.0 / HALF_WIDTH

N = 16
C = 8
X = 128
NPR = 64
SHARD = 32
NP = 256
CHUNK = 8
F32 = jnp.float32
BF16 = jnp.bfloat16
MESH = pl.DeviceIdType.MESH
ANY = pl.BlockSpec(memory_space=pl.ANY)
SMEM = pl.BlockSpec(memory_space=pltpu.SMEM)


def split(value):
    high = value.astype(BF16)
    return high, (value - high.astype(F32)).astype(BF16)


def same_layer(rows, columns):
    row = lax.broadcasted_iota(jnp.int32, (rows, columns), 0)
    column = lax.broadcasted_iota(jnp.int32, (rows, columns), 1)
    return (row & 7) == (column & 7)


def dot(left, right):
    return jnp.dot(left, right, preferred_element_type=F32)


def convert(source, target, first, count):
    @pl.loop(0, count // 16)
    def _(step):
        start = pl.multiple_of(first + step * 16, 8)
        row = pl.multiple_of(start * 8, 64)
        for y in range(C):
            rows = source[pl.ds(start, 16), y * 8 : y * 8 + 8, :].reshape(128, X)
            high, low = split(rows)
            target[pl.ds(row, 128), y * X : (y + 1) * X] = high
            target[pl.ds(row, 128), (C + y) * X : (C + y + 1) * X] = low


def transpose_block(source, target):
    for y in range(C):
        rows = source[:, y * 8 : y * 8 + 8, :].reshape(N * 8, X).T
        high, low = split(rows)
        target[y * X : (y + 1) * X, 0:128] = high
        target[y * X : (y + 1) * X, 128:256] = low


def contract(table, block, sums, first, count):
    @pl.loop(0, count // 32)
    def _(step):
        start = pl.multiple_of(first + step * 32, 32)
        rows = pl.ds(pl.multiple_of(start * 8, 256), 256)
        full = dot(table[rows, 0:1024], block[...]) + dot(table[rows, 1024:2048], block[...])
        both = full[:, 0:128] + full[:, 128:256]
        kept = jnp.where(same_layer(256, 128), both, 0.0)
        sums[pl.ds(start, 32), :] = kept.reshape(32, 8, 128).sum(axis=1)


def fold_layers(sums):
    band = lax.broadcasted_iota(jnp.int32, (N, 128), 0)
    column = lax.broadcasted_iota(jnp.int32, (N, 128), 1)
    ones = jnp.where(band == (column >> 3), 1.0, 0.0).astype(F32)
    return lax.dot_general(
        ones,
        sums,
        (((1,), (1,)), ((), ())),
        precision=lax.Precision.HIGHEST,
        preferred_element_type=F32,
    )


def spread(coefs, repeat, target, columns):
    count = coefs.shape[1]
    wide = jnp.broadcast_to(coefs[:, None, :], (N, 8, count)).reshape(N * 8, count)
    high, low = split(wide)
    both = jnp.concatenate([high, low], axis=0)
    for at in range(0, columns, 256):
        values = dot(both, repeat[0:count, at : at + 256])
        target[:, at : at + 256] = jnp.where(same_layer(256, 256), values, 0.0).astype(BF16)


def kernel(
    prev_hbm, cur_hbm, pot_hbm, proj_hbm, coup, pattern, counts, pan_hbm,
    out_hbm, coef_out,
    cur, turned, y_low, y_high, z_low, z_high, filt, prev, pot, proj, proj_split,
    gathered, pan_split, block, repeat, spread_ref, sums, small_a, small_b, coef_a, coef_b,
    load_sem, halo_send, halo_recv, right_send, left_recv, left_send, right_recv,
    sib_send, sib_recv, ahead_send, behind_recv, back_send, front_recv,
    sum_send, sum_recv, store_sem,
):
    gy, gz, band = lax.axis_index("gy"), lax.axis_index("gz"), lax.axis_index("band")
    z_hi, y = gy // 8, gy % 8
    z = z_hi * 4 + gz
    x, core = band // 2, band % 2

    def at_y(other):
        return {"gy": z_hi * 8 + other, "gz": gz, "band": band}

    def at_z(other):
        return {"gy": (other // 4) * 8 + y, "gz": other % 4, "band": band}

    def at_band(other):
        return {"gy": gy, "gz": gz, "band": other}

    up_y = {"gy": (gy + 1) % 16, "gz": gz, "band": band}
    down_y = {"gy": (gy + 15) % 16, "gz": gz, "band": band}
    up_z = {"gy": gy, "gz": (gz + 1) % 4, "band": band}
    down_z = {"gy": gy, "gz": (gz + 3) % 4, "band": band}
    right, left = ((x + 1) % 4) * 2 + core, ((x + 3) % 4) * 2 + core
    opposite, sibling = ((x + 2) % 4) * 2 + core, x * 2 + 1 - core

    own_rows = pl.ds(pl.multiple_of(band * SHARD, SHARD), SHARD)
    load_pan = pltpu.make_async_copy(pan_hbm, gathered.at[own_rows], load_sem.at[0])
    load_cur = pltpu.make_async_copy(cur_hbm, cur, load_sem.at[1])
    load_proj = pltpu.make_async_copy(proj_hbm, proj, load_sem.at[2])
    load_prev = pltpu.make_async_copy(prev_hbm, prev, load_sem.at[3])
    load_pot = pltpu.make_async_copy(pot_hbm, pot, load_sem.at[4])
    for load in (load_pan, load_cur, load_proj, load_prev, load_pot):
        load.start()

    barrier = pltpu.get_barrier_semaphore()
    partners = [at_y((y + r) % 8) for r in range(1, 8)]
    partners += [at_z((z + r) % 8) for r in range(1, 8)]
    partners += [up_y, down_y, up_z, down_z]
    partners += [at_band(right), at_band(left), at_band(sibling)]
    for partner in partners:
        pl.semaphore_signal(barrier, inc=1, device_id=partner, device_id_type=MESH)
    pl.semaphore_wait(barrier, len(partners))

    def remote(source, target, send, recv, device):
        return pltpu.make_async_remote_copy(
            src_ref=source, dst_ref=target, send_sem=send, recv_sem=recv,
            device_id=device, device_id_type=MESH,
        )

    def panel_copy(owner, k, send, recv, device):
        rows = gathered.at[pl.ds(pl.multiple_of(owner * SHARD + k * CHUNK, CHUNK), CHUNK)]
        return remote(rows, rows, send, recv, device)

    load_pan.wait()
    started = []
    for step in range(4):
        k = step
        started.append(panel_copy(band, k, right_send.at[k], left_recv.at[k], at_band(right)))
        started[-1].start()
        k = (step + 2) % 4
        started.append(panel_copy(band, k, left_send.at[k], right_recv.at[k], at_band(left)))
        started[-1].start()
    for k in range(4):
        started.append(panel_copy(band, k, sib_send.at[k], sib_recv.at[k], at_band(sibling)))
        started[-1].start()

    load_cur.wait()
    halo_y0 = remote(cur.at[:, pl.ds(16, 48)], y_low, halo_send.at[0], halo_recv.at[0], up_y)
    halo_y1 = remote(cur.at[:, pl.ds(0, 48)], y_high, halo_send.at[1], halo_recv.at[1], down_y)
    halo_y0.start()
    halo_y1.start()

    @pl.loop(0, N)
    def _(n):
        for layer in range(C):
            turned[n, layer * 8 : layer * 8 + 8, :] = cur[n, pl.ds(layer, 8, stride=8), :]

    halo_z0 = remote(turned.at[:, pl.ds(16, 48)], z_low, halo_send.at[2], halo_recv.at[2], up_z)
    halo_z1 = remote(turned.at[:, pl.ds(0, 48)], z_high, halo_send.at[3], halo_recv.at[3], down_z)
    halo_z0.start()
    halo_z1.start()

    transpose_block(cur, block)
    load_proj.wait()
    convert(proj, proj_split, 0, NPR)
    contract(proj_split, block, sums, 0, NPR)
    sums[NPR:128, :] = jnp.zeros((128 - NPR, 128), F32)

    lane = lax.broadcasted_iota(jnp.int32, (N, 128), 1)
    tile = gy * 4 + gz
    weight = jnp.zeros((N, 128), F32)
    for b in range(8):
        reached = pattern[b, tile].astype(F32)
        live = ((lane >> 3) == b) & ((lane & 7) < counts[b])
        weight = jnp.where(live, reached, weight)
    coupling = jnp.zeros((N, 128), F32)
    for j in range(NPR):
        coupling = jnp.where(lane == j, coup[j], coupling)

    def send_y(buffer, sems):
        copies = []
        for r in range(1, 8):
            copies.append(
                remote(buffer.at[y], buffer.at[y], sum_send.at[sems, r], sum_recv.at[sems, y], at_y((y + r) % 8))
            )
            copies[-1].start()
        return copies

    def send_z(buffer, sems):
        copies = []
        for r in range(1, 8):
            copies.append(
                remote(buffer.at[z], buffer.at[z], sum_send.at[sems, r], sum_recv.at[sems, z], at_z((z + r) % 8))
            )
            copies[-1].start()
        return copies

    def receive(buffer, sems, me):
        for r in range(1, 8):
            other = (me + r) % 8
            remote(buffer.at[other], buffer.at[other], sum_send.at[sems, r], sum_recv.at[sems, other], up_y).wait_recv()

    def total(buffer):
        value = buffer[0]
        for i in range(1, 8):
            value = value + buffer[i]
        return value

    small_a[y] = fold_layers(sums[0:128, :]) * weight
    sent = send_y(small_a, 0)

    load_prev.wait()
    load_pot.wait()

    @pl.loop(0, N)
    def _(n):
        value = cur[n]
        lap = 3.0 * STENCIL[0] * value
        for reach in range(1, 7):
            lap = lap + STENCIL[reach] * (pltpu.roll(value, reach, 1) + pltpu.roll(value, X - reach, 1))
        filt[n] = SCALE * (-0.5 * lap + pot[...] * value - CENTER * value) - prev[n]

    receive(small_a, 0, y)
    small_b[z] = total(small_a)
    sent += send_z(small_b, 1)

    @pl.loop(0, 8)
    def _(step):
        at = pl.multiple_of(step * 256, 256)
        row = lax.broadcasted_iota(jnp.int32, (NP, 256), 0)
        column = lax.broadcasted_iota(jnp.int32, (NP, 256), 1) + at
        repeat[:, pl.ds(at, 256)] = jnp.where(row == (column >> 3), 1.0, 0.0).astype(BF16)

    own_first = pl.multiple_of(band * SHARD, SHARD)
    convert(gathered, pan_split, own_first, SHARD)

    receive(small_b, 1, z)
    spread(total(small_b) * (coupling * weight), repeat, spread_ref, 512)
    for part in range(4):
        at = part * 256
        value = dot(spread_ref[:, 0:512], proj_split[:, at : at + 256])
        value = value[0:128] + value[128:256] + dot(spread_ref[0:128, 0:512], proj_split[:, 1024 + at : 1280 + at])
        for half in range(2):
            rows = pl.ds((part * 2 + half) * 8, 8)
            filt[:, rows, :] += SCALE * value[:, half * X : (half + 1) * X].reshape(N, 8, X)

    def pass_on(copy):
        copy.start()
        started.append(copy)

    for step in range(4):
        k = step
        panel_copy(left, k, right_send.at[k], left_recv.at[k], at_band(right)).wait_recv()
        if k < 2:
            pass_on(panel_copy(left, k, ahead_send.at[k], behind_recv.at[k], at_band(right)))
        pass_on(panel_copy(left, k, sib_send.at[4 + k], sib_recv.at[4 + k], at_band(sibling)))
        k = (step + 2) % 4
        panel_copy(right, k, left_send.at[k], right_recv.at[k], at_band(left)).wait_recv()
        if k >= 2:
            pass_on(panel_copy(right, k, back_send.at[k - 2], front_recv.at[k - 2], at_band(left)))
        pass_on(panel_copy(right, k, sib_send.at[8 + k], sib_recv.at[8 + k], at_band(sibling)))

    def take(owner, slot):
        for k in range(4):
            panel_copy(owner, k, sib_send.at[slot + k], sib_recv.at[slot + k], at_band(sibling)).wait_recv()

    def other_core(owner):
        return owner + 1 - 2 * core

    def convert_shard(owner):
        convert(gathered, pan_split, pl.multiple_of(owner * SHARD, SHARD), SHARD)

    take(sibling, 0)
    convert_shard(sibling)
    convert_shard(left)
    convert_shard(right)
    take(other_core(left), 4)
    convert_shard(other_core(left))
    take(other_core(right), 8)
    convert_shard(other_core(right))

    halo_y0.wait_recv()
    halo_y1.wait_recv()

    def stencil(rows):
        result = []
        for at in range(C):
            value = None
            for reach in range(1, 7):
                pair = STENCIL[reach] * (rows[6 + at + reach] + rows[6 + at - reach])
                value = pair if value is None else value + pair
            result.append(-0.5 * SCALE * value)
        return result

    def lines(ref, n, count):
        return [ref[n, i * 8 : i * 8 + 8, :] for i in range(count)]

    @pl.loop(0, N)
    def _(n):
        parts = stencil(lines(y_low, n, 6) + lines(cur, n, 8) + lines(y_high, n, 6))
        for at in range(C):
            filt[n, at * 8 : at * 8 + 8, :] += parts[at]

    halo_z0.wait_recv()
    halo_z1.wait_recv()

    @pl.loop(0, N)
    def _(n):
        parts = stencil(lines(z_low, n, 6) + lines(turned, n, 8) + lines(z_high, n, 6))
        for at in range(C):
            filt[n, pl.ds(at, 8, stride=8), :] += parts[at]

    transpose_block(filt, block)

    for k in (0, 1):
        panel_copy(opposite, k, ahead_send.at[k], behind_recv.at[k], at_band(right)).wait_recv()
        pass_on(panel_copy(opposite, k, sib_send.at[12 + k], sib_recv.at[12 + k], at_band(sibling)))
        panel_copy(opposite, k + 2, back_send.at[k], front_recv.at[k], at_band(left)).wait_recv()
        pass_on(panel_copy(opposite, k + 2, sib_send.at[14 + k], sib_recv.at[14 + k], at_band(sibling)))
    convert_shard(opposite)
    take(other_core(opposite), 12)
    convert_shard(other_core(opposite))

    contract(pan_split, block, sums, 0, NP)
    coef_a[y] = fold_layers(sums[...])
    sent += send_y(coef_a, 2)
    receive(coef_a, 2, y)
    coef_b[z] = total(coef_a)
    sent += send_z(coef_b, 3)
    receive(coef_b, 3, z)
    coefs = total(coef_b)
    coef_out[...] = coefs
    spread(coefs, repeat, spread_ref, 2048)
    stores = []
    for part in range(4):
        at = part * 256
        value = dot(spread_ref[...], pan_split[:, at : at + 256])
        value = value[0:128] + value[128:256] + dot(spread_ref[0:128, :], pan_split[:, 1024 + at : 1280 + at])
        for half in range(2):
            rows = pl.ds((part * 2 + half) * 8, 8)
            filt[:, rows, :] -= value[:, half * X : (half + 1) * X].reshape(N, 8, X)
        rows = pl.ds(part * 16, 16)
        stores.append(pltpu.make_async_copy(filt.at[:, rows], out_hbm.at[:, rows], store_sem.at[part]))
        stores[-1].start()

    for copy in started + sent + [halo_y0, halo_y1, halo_z0, halo_z1]:
        copy.wait_send()
    for copy in stores:
        copy.wait()


def per_device(previous, current, potential, projectors, couplings, pattern, counts, panels):
    rows = C * C
    vmem = pltpu.VMEM
    dma = pltpu.SemaphoreType.DMA
    rotated, coefs = pl.pallas_call(
        kernel,
        out_shape=(
            jax.ShapeDtypeStruct((N, rows, X), F32),
            jax.ShapeDtypeStruct((N, NP), F32),
        ),
        in_specs=[ANY, ANY, ANY, ANY, SMEM, SMEM, SMEM, ANY],
        out_specs=(ANY, pl.BlockSpec(memory_space=pltpu.VMEM)),
        scratch_shapes=[
            vmem((N, rows, X), F32),
            vmem((N, rows, X), F32),
            vmem((N, 48, X), F32),
            vmem((N, 48, X), F32),
            vmem((N, 48, X), F32),
            vmem((N, 48, X), F32),
            vmem((N, rows, X), F32),
            vmem((N, rows, X), F32),
            vmem((rows, X), F32),
            vmem((NPR, rows, X), F32),
            vmem((NPR * 8, 2048), BF16),
            vmem((NP, rows, X), F32),
            vmem((NP * 8, 2048), BF16),
            vmem((1024, 256), BF16),
            vmem((NP, 2048), BF16),
            vmem((256, 2048), BF16),
            vmem((NP, 128), F32),
            vmem((8, N, 128), F32),
            vmem((8, N, 128), F32),
            vmem((8, N, NP), F32),
            vmem((8, N, NP), F32),
            dma((5,)),
            dma((4,)),
            dma((4,)),
            dma((4,)),
            dma((4,)),
            dma((4,)),
            dma((4,)),
            dma((16,)),
            dma((16,)),
            dma((2,)),
            dma((2,)),
            dma((2,)),
            dma((2,)),
            dma((4, 8)),
            dma((4, 8)),
            dma((4,)),
        ],
        compiler_params=pltpu.CompilerParams(
            collective_id=0, has_side_effects=True, vmem_limit_bytes=56 * 1024 * 1024
        ),
        cost_estimate=pl.CostEstimate(flops=10**9, bytes_accessed=5 * 2**20, transcendentals=0),
        name="filter_step",
    )(
        previous.reshape(N, rows, X),
        current.reshape(N, rows, X),
        potential.reshape(rows, X),
        projectors.reshape(NPR, rows, X),
        couplings,
        pattern,
        counts,
        panels.reshape(SHARD, rows, X),
    )
    return rotated.reshape(N, C, C, X), coefs.T


def solution(mesh):
    in_specs = (
        P("band", "gy", "gz", None),
        P("band", "gy", "gz", None),
        P("gy", "gz", None),
        P(None, "gy", "gz", None),
        P(),
        P(),
        P(),
        P("band", "gy", "gz", None),
    )
    out_specs = (P("band", "gy", "gz", None), P(None, "band"))
    return jax.shard_map(
        per_device, mesh=mesh, in_specs=in_specs, out_specs=out_specs, check_vma=False
    )
```

time: 709 us -> 91.4 us (0.13)
  the two profiles are of different devices: /device:TPU:38 before, /device:TPU:1 now
where the time goes in v1:
time: 91.4 us; the launch traced here: 91.2 us
  Pallas kernels  87.3 us (96%)
  local copies, waits for them, and re-layouts  3.21 us (4%)
    pallas_call x1, Pallas kernels, per_device(): pl.pallas_call(kernel, out_shape=(jax.ShapeDtypeStruct((N, rows, X), F32)...  87.3 us
    unnamed x2, local copies, waits for them, and re-layouts  3.21 us

profile of v1, /device:TPU:1, one launch (start us, length us, event | category | flops | bytes accessed | tf_op | source)
XLA Modules:
  0.0 91.2 jit_solution(345988826680584769)
XLA Ops:
  0.6 87.3 %filter_step.1 = (f32[16,64,128]{2,1,0:T(8,128)}, f32[16,256]{1,0:T(8,128)}) custom-call(f32[16,64,128]{2,1,0:T(8,128)} %bitcast.10, f32[16,64,128]{2,1,0:T(8,128)} %bitcast.11, f32[64,128]{1,0:T(8,128)} %bitcast.12, f32[64,64,128]{2,1,0:T(8,128)} %bitcast.7, f32[64]{0:T(128)} %coup.1, s32[8,64]{1,0:T(8,128)} %pattern.1, s32[8]{0:T(128)} %counts.1, ...), custom_call_target="tpu_custom_call" | custom-call | flops 1000000000 | bytes 5242880 | tf_op jit(solution)/shard_map/filter_step/pallas_call | solution.py:384
  88.0 1.9 %copy.12 = f32[16,8,8,128]{3,2,1,0:T(8,128)} copy(f32[16,8,8,128]{3,2,1,0:T(8,128)} %bitcast.9) | data formatting | bytes 1048576
  89.9 1.3 %copy.13 = f32[256,16]{0,1:T(8,128)} copy(f32[256,16]{0,1:T(8,128)} %bitcast.13) | data formatting | bytes 32768

commit v2 on v1

--- a/solution.py
+++ b/solution.py
@@ -24,6 +24,7 @@
 NPR = 64
 SHARD = 32
 NP = 256
+NEAR = 192
 CHUNK = 8
 F32 = jnp.float32
 BF16 = jnp.bfloat16
@@ -91,21 +92,30 @@
     )
 
 
-def spread(coefs, repeat, target, columns):
+def pack(coefs):
+    return jnp.concatenate([coefs[0:8], coefs[8:16]], axis=1)
+
+
+def unpack(packed):
+    return jnp.concatenate([packed[:, 0:64], packed[:, 64:128]], axis=0)
+
+
+def spread(coefs, repeat, target, first):
     count = coefs.shape[1]
+    columns = count * 8
     wide = jnp.broadcast_to(coefs[:, None, :], (N, 8, count)).reshape(N * 8, count)
     high, low = split(wide)
     both = jnp.concatenate([high, low], axis=0)
     for at in range(0, columns, 256):
         values = dot(both, repeat[0:count, at : at + 256])
-        target[:, at : at + 256] = jnp.where(same_layer(256, 256), values, 0.0).astype(BF16)
+        target[:, first + at : first + at + 256] = jnp.where(same_layer(256, 256), values, 0.0).astype(BF16)
 
 
 def kernel(
     prev_hbm, cur_hbm, pot_hbm, proj_hbm, coup, pattern, counts, pan_hbm,
     out_hbm, coef_out,
     cur, turned, y_low, y_high, z_low, z_high, filt, prev, pot, proj, proj_split,
-    gathered, pan_split, block, repeat, spread_ref, sums, small_a, small_b, coef_a, coef_b,
+    gathered, pan_split, block, repeat, spread_ref, sums, small_a, small_b, near_a, near_b, far_a, far_b,
     load_sem, halo_send, halo_recv, right_send, left_recv, left_send, right_recv,
     sib_send, sib_recv, ahead_send, behind_recv, back_send, front_recv,
     sum_send, sum_recv, store_sem,
@@ -131,8 +141,11 @@
     right, left = ((x + 1) % 4) * 2 + core, ((x + 3) % 4) * 2 + core
     opposite, sibling = ((x + 2) % 4) * 2 + core, x * 2 + 1 - core
 
-    own_rows = pl.ds(pl.multiple_of(band * SHARD, SHARD), SHARD)
-    load_pan = pltpu.make_async_copy(pan_hbm, gathered.at[own_rows], load_sem.at[0])
+    own_at, right_at, left_at, opposite_at = 0, 2, 4, 6
+    owners = [band, sibling]
+    for chip in (right, left, opposite):
+        owners += [chip, chip + 1 - 2 * core]
+    load_pan = pltpu.make_async_copy(pan_hbm, gathered.at[pl.ds(0, SHARD)], load_sem.at[0])
     load_cur = pltpu.make_async_copy(cur_hbm, cur, load_sem.at[1])
     load_proj = pltpu.make_async_copy(proj_hbm, proj, load_sem.at[2])
     load_prev = pltpu.make_async_copy(prev_hbm, prev, load_sem.at[3])
@@ -155,22 +168,35 @@
             device_id=device, device_id_type=MESH,
         )
 
-    def panel_copy(owner, k, send, recv, device):
-        rows = gathered.at[pl.ds(pl.multiple_of(owner * SHARD + k * CHUNK, CHUNK), CHUNK)]
-        return remote(rows, rows, send, recv, device)
+    def panel_copy(slot, there, k, send, recv, device):
+        source = gathered.at[pl.ds(slot * SHARD + k * CHUNK, CHUNK)]
+        target = gathered.at[pl.ds(there * SHARD + k * CHUNK, CHUNK)]
+        return remote(source, target, send, recv, device)
+
+    def to_right(slot, there, k, sems, recvs, at):
+        return panel_copy(slot, there, k, sems.at[at], recvs.at[at], at_band(right))
+
+    def to_left(slot, there, k, sems, recvs, at):
+        return panel_copy(slot, there, k, sems.at[at], recvs.at[at], at_band(left))
+
+    def to_sibling(slot, k):
+        at = slot // 2 * 4 + k
+        return panel_copy(slot, slot + 1, k, sib_send.at[at], sib_recv.at[at], at_band(sibling))
 
     load_pan.wait()
     started = []
+
+    def pass_on(copy):
+        copy.start()
+        started.append(copy)
+
     for step in range(4):
         k = step
-        started.append(panel_copy(band, k, right_send.at[k], left_recv.at[k], at_band(right)))
-        started[-1].start()
+        pass_on(to_right(own_at, left_at, k, right_send, left_recv, k))
         k = (step + 2) % 4
-        started.append(panel_copy(band, k, left_send.at[k], right_recv.at[k], at_band(left)))
-        started[-1].start()
+        pass_on(to_left(own_at, right_at, k, left_send, right_recv, k))
     for k in range(4):
-        started.append(panel_copy(band, k, sib_send.at[k], sib_recv.at[k], at_band(sibling)))
-        started[-1].start()
+        pass_on(to_sibling(own_at, k))
 
     load_cur.wait()
     halo_y0 = remote(cur.at[:, pl.ds(16, 48)], y_low, halo_send.at[0], halo_recv.at[0], up_y)
@@ -192,16 +218,15 @@
     load_proj.wait()
     convert(proj, proj_split, 0, NPR)
     contract(proj_split, block, sums, 0, NPR)
-    sums[NPR:128, :] = jnp.zeros((128 - NPR, 128), F32)
-
-    lane = lax.broadcasted_iota(jnp.int32, (N, 128), 1)
+
+    lane = lax.broadcasted_iota(jnp.int32, (N, NPR), 1)
     tile = gy * 4 + gz
-    weight = jnp.zeros((N, 128), F32)
+    weight = jnp.zeros((N, NPR), F32)
     for b in range(8):
         reached = pattern[b, tile].astype(F32)
         live = ((lane >> 3) == b) & ((lane & 7) < counts[b])
         weight = jnp.where(live, reached, weight)
-    coupling = jnp.zeros((N, 128), F32)
+    coupling = jnp.zeros((N, NPR), F32)
     for j in range(NPR):
         coupling = jnp.where(lane == j, coup[j], coupling)
 
@@ -234,7 +259,7 @@
             value = value + buffer[i]
         return value
 
-    small_a[y] = fold_layers(sums[0:128, :]) * weight
+    small_a[y] = pack(fold_layers(sums[0:NPR, :]) * weight)
     sent = send_y(small_a, 0)
 
     load_prev.wait()
@@ -252,18 +277,38 @@
     small_b[z] = total(small_a)
     sent += send_z(small_b, 1)
 
-    @pl.loop(0, 8)
+    @pl.loop(0, 6)
     def _(step):
         at = pl.multiple_of(step * 256, 256)
-        row = lax.broadcasted_iota(jnp.int32, (NP, 256), 0)
-        column = lax.broadcasted_iota(jnp.int32, (NP, 256), 1) + at
+        row = lax.broadcasted_iota(jnp.int32, (NEAR, 256), 0)
+        column = lax.broadcasted_iota(jnp.int32, (NEAR, 256), 1) + at
         repeat[:, pl.ds(at, 256)] = jnp.where(row == (column >> 3), 1.0, 0.0).astype(BF16)
 
-    own_first = pl.multiple_of(band * SHARD, SHARD)
-    convert(gathered, pan_split, own_first, SHARD)
+    convert(gathered, pan_split, 0, SHARD)
+
+    for step in range(4):
+        k = step
+        to_right(own_at, left_at, k, right_send, left_recv, k).wait_recv()
+        if k < 2:
+            pass_on(to_right(left_at, opposite_at, k, ahead_send, behind_recv, k))
+        pass_on(to_sibling(left_at, k))
+        k = (step + 2) % 4
+        to_left(own_at, right_at, k, left_send, right_recv, k).wait_recv()
+        if k >= 2:
+            pass_on(to_left(right_at, opposite_at, k, back_send, front_recv, k - 2))
+        pass_on(to_sibling(right_at, k))
+
+    def take(slot):
+        for k in range(4):
+            to_sibling(slot, k).wait_recv()
+
+    take(own_at)
+    convert(gathered, pan_split, SHARD, SHARD)
+    convert(gathered, pan_split, right_at * SHARD, SHARD)
+    convert(gathered, pan_split, left_at * SHARD, SHARD)
 
     receive(small_b, 1, z)
-    spread(total(small_b) * (coupling * weight), repeat, spread_ref, 512)
+    spread(unpack(total(small_b)) * (coupling * weight), repeat, spread_ref, 0)
     for part in range(4):
         at = part * 256
         value = dot(spread_ref[:, 0:512], proj_split[:, at : at + 256])
@@ -272,40 +317,10 @@
             rows = pl.ds((part * 2 + half) * 8, 8)
             filt[:, rows, :] += SCALE * value[:, half * X : (half + 1) * X].reshape(N, 8, X)
 
-    def pass_on(copy):
-        copy.start()
-        started.append(copy)
-
-    for step in range(4):
-        k = step
-        panel_copy(left, k, right_send.at[k], left_recv.at[k], at_band(right)).wait_recv()
-        if k < 2:
-            pass_on(panel_copy(left, k, ahead_send.at[k], behind_recv.at[k], at_band(right)))
-        pass_on(panel_copy(left, k, sib_send.at[4 + k], sib_recv.at[4 + k], at_band(sibling)))
-        k = (step + 2) % 4
-        panel_copy(right, k, left_send.at[k], right_recv.at[k], at_band(left)).wait_recv()
-        if k >= 2:
-            pass_on(panel_copy(right, k, back_send.at[k - 2], front_recv.at[k - 2], at_band(left)))
-        pass_on(panel_copy(right, k, sib_send.at[8 + k], sib_recv.at[8 + k], at_band(sibling)))
-
-    def take(owner, slot):
-        for k in range(4):
-            panel_copy(owner, k, sib_send.at[slot + k], sib_recv.at[slot + k], at_band(sibling)).wait_recv()
-
-    def other_core(owner):
-        return owner + 1 - 2 * core
-
-    def convert_shard(owner):
-        convert(gathered, pan_split, pl.multiple_of(owner * SHARD, SHARD), SHARD)
-
-    take(sibling, 0)
-    convert_shard(sibling)
-    convert_shard(left)
-    convert_shard(right)
-    take(other_core(left), 4)
-    convert_shard(other_core(left))
-    take(other_core(right), 8)
-    convert_shard(other_core(right))
+    take(right_at)
+    convert(gathered, pan_split, (right_at + 1) * SHARD, SHARD)
+    take(left_at)
+    convert(gathered, pan_split, (left_at + 1) * SHARD, SHARD)
 
     halo_y0.wait_recv()
     halo_y1.wait_recv()
@@ -329,6 +344,12 @@
         for at in range(C):
             filt[n, at * 8 : at * 8 + 8, :] += parts[at]
 
+    for k in (0, 1):
+        to_right(left_at, opposite_at, k, ahead_send, behind_recv, k).wait_recv()
+        pass_on(to_sibling(opposite_at, k))
+        to_left(right_at, opposite_at, k + 2, back_send, front_recv, k).wait_recv()
+        pass_on(to_sibling(opposite_at, k + 2))
+
     halo_z0.wait_recv()
     halo_z1.wait_recv()
 
@@ -340,36 +361,56 @@
 
     transpose_block(filt, block)
 
-    for k in (0, 1):
-        panel_copy(opposite, k, ahead_send.at[k], behind_recv.at[k], at_band(right)).wait_recv()
-        pass_on(panel_copy(opposite, k, sib_send.at[12 + k], sib_recv.at[12 + k], at_band(sibling)))
-        panel_copy(opposite, k + 2, back_send.at[k], front_recv.at[k], at_band(left)).wait_recv()
-        pass_on(panel_copy(opposite, k + 2, sib_send.at[14 + k], sib_recv.at[14 + k], at_band(sibling)))
-    convert_shard(opposite)
-    take(other_core(opposite), 12)
-    convert_shard(other_core(opposite))
-
-    contract(pan_split, block, sums, 0, NP)
-    coef_a[y] = fold_layers(sums[...])
-    sent += send_y(coef_a, 2)
-    receive(coef_a, 2, y)
-    coef_b[z] = total(coef_a)
-    sent += send_z(coef_b, 3)
-    receive(coef_b, 3, z)
-    coefs = total(coef_b)
-    coef_out[...] = coefs
-    spread(coefs, repeat, spread_ref, 2048)
-    stores = []
-    for part in range(4):
+    contract(pan_split, block, sums, 0, NEAR)
+    near = fold_layers(sums[0:NEAR, :])
+    near_a[y, 0:16, :] = near[:, 0:128]
+    near_a[y, 16:24, :] = pack(near[:, 128:NEAR])
+    sent += send_y(near_a, 2)
+    convert(gathered, pan_split, opposite_at * SHARD, SHARD)
+    take(opposite_at)
+    convert(gathered, pan_split, (opposite_at + 1) * SHARD, SHARD)
+    contract(pan_split, block, sums, NEAR, NP - NEAR)
+    far_a[y] = pack(fold_layers(sums[NEAR:NP, :]))
+    sent += send_y(far_a, 3)
+    receive(near_a, 2, y)
+    near_b[z] = total(near_a)
+    sent += send_z(near_b, 4)
+    receive(far_a, 3, y)
+    far_b[z] = total(far_a)
+    sent += send_z(far_b, 5)
+
+    def take_away(first, count, part):
         at = part * 256
-        value = dot(spread_ref[...], pan_split[:, at : at + 256])
-        value = value[0:128] + value[128:256] + dot(spread_ref[0:128, :], pan_split[:, 1024 + at : 1280 + at])
+        table = pl.ds(first * 8, count * 8)
+        value = dot(spread_ref[:, table], pan_split[table, at : at + 256])
+        value = value[0:128] + value[128:256] + dot(spread_ref[0:128, table], pan_split[table, 1024 + at : 1280 + at])
         for half in range(2):
             rows = pl.ds((part * 2 + half) * 8, 8)
             filt[:, rows, :] -= value[:, half * X : (half + 1) * X].reshape(N, 8, X)
+
+    def write_coefs(coefs, slot):
+        values = coefs.T
+        for i in range(coefs.shape[1] // SHARD):
+            rows = pl.ds(pl.multiple_of(owners[slot + i] * SHARD, SHARD), SHARD)
+            coef_out[rows, :] = values[i * SHARD : (i + 1) * SHARD, :]
+
+    receive(near_b, 4, z)
+    packed = total(near_b)
+    near = jnp.concatenate([packed[0:16], unpack(packed[16:24])], axis=1)
+    spread(near, repeat, spread_ref, 0)
+    for part in range(4):
+        take_away(0, NEAR, part)
+    write_coefs(near, 0)
+    receive(far_b, 5, z)
+    far = unpack(total(far_b))
+    spread(far, repeat, spread_ref, NEAR * 8)
+    stores = []
+    for part in range(4):
+        take_away(NEAR, NP - NEAR, part)
         rows = pl.ds(part * 16, 16)
         stores.append(pltpu.make_async_copy(filt.at[:, rows], out_hbm.at[:, rows], store_sem.at[part]))
         stores[-1].start()
+    write_coefs(far, opposite_at)
 
     for copy in started + sent + [halo_y0, halo_y1, halo_z0, halo_z1]:
         copy.wait_send()
@@ -385,7 +426,7 @@
         kernel,
         out_shape=(
             jax.ShapeDtypeStruct((N, rows, X), F32),
-            jax.ShapeDtypeStruct((N, NP), F32),
+            jax.ShapeDtypeStruct((NP, N), F32),
         ),
         in_specs=[ANY, ANY, ANY, ANY, SMEM, SMEM, SMEM, ANY],
         out_specs=(ANY, pl.BlockSpec(memory_space=pltpu.VMEM)),
@@ -404,13 +445,15 @@
             vmem((NP, rows, X), F32),
             vmem((NP * 8, 2048), BF16),
             vmem((1024, 256), BF16),
-            vmem((NP, 2048), BF16),
+            vmem((NEAR, 1536), BF16),
             vmem((256, 2048), BF16),
             vmem((NP, 128), F32),
-            vmem((8, N, 128), F32),
-            vmem((8, N, 128), F32),
-            vmem((8, N, NP), F32),
-            vmem((8, N, NP), F32),
+            vmem((8, 8, 128), F32),
+            vmem((8, 8, 128), F32),
+            vmem((8, 24, 128), F32),
+            vmem((8, 24, 128), F32),
+            vmem((8, 8, 128), F32),
+            vmem((8, 8, 128), F32),
             dma((5,)),
             dma((4,)),
             dma((4,)),
@@ -424,8 +467,8 @@
             dma((2,)),
             dma((2,)),
             dma((2,)),
-            dma((4, 8)),
-            dma((4, 8)),
+            dma((6, 8)),
+            dma((6, 8)),
             dma((4,)),
         ],
         compiler_params=pltpu.CompilerParams(
@@ -443,7 +486,7 @@
         counts,
         panels.reshape(SHARD, rows, X),
     )
-    return rotated.reshape(N, C, C, X), coefs.T
+    return rotated.reshape(N, C, C, X), coefs
 
 
 def solution(mesh):

time: 91.4 us -> 76.8 us (0.84)
  the two profiles are of different devices: /device:TPU:1 before, /device:TPU:18 now
where the time goes in v2:
time: 76.8 us; the launch traced here: 76.5 us
  Pallas kernels  72.4 us (94%)
  local copies, waits for them, and re-layouts  3.46 us (5%)
    pallas_call x1, Pallas kernels, per_device(): pl.pallas_call(kernel, out_shape=(jax.ShapeDtypeStruct((N, rows, X), F32)...  72.4 us
    unnamed x2, local copies, waits for them, and re-layouts  3.46 us

profile of v2, /device:TPU:18, one launch (start us, length us, event | category | flops | bytes accessed | tf_op | source)
XLA Modules:
  0.0 76.5 jit_solution(11743946989853344411)
XLA Ops:
  0.6 72.4 %filter_step.1 = (f32[16,64,128]{2,1,0:T(8,128)}, f32[256,16]{1,0:T(8,128)}) custom-call(f32[16,64,128]{2,1,0:T(8,128)} %bitcast.9, f32[16,64,128]{2,1,0:T(8,128)} %bitcast.10, f32[64,128]{1,0:T(8,128)} %bitcast.11, f32[64,64,128]{2,1,0:T(8,128)} %bitcast.6, f32[64]{0:T(128)} %coup.1, s32[8,64]{1,0:T(8,128)} %pattern.1, s32[8]{0:T(128)} %counts.1, ...), custom_call_target="tpu_custom_call" | custom-call | flops 1000000000 | bytes 5242880 | tf_op jit(solution)/shard_map/filter_step/pallas_call | solution.py:425
  73.1 1.6 %copy.10 = f32[256,16]{0,1:T(8,128)} copy(f32[256,16]{1,0:T(8,128)} %get-tuple-element.7) | data formatting | bytes 32768
  74.7 1.9 %copy.12 = f32[16,8,8,128]{3,2,1,0:T(8,128)} copy(f32[16,8,8,128]{3,2,1,0:T(8,128)} %bitcast.8) | data formatting | bytes 1048576

commit v3 on v2

--- a/solution.py
+++ b/solution.py
@@ -26,6 +26,7 @@
 NP = 256
 NEAR = 192
 CHUNK = 8
+DIRECT = 8
 F32 = jnp.float32
 BF16 = jnp.bfloat16
 MESH = pl.DeviceIdType.MESH
@@ -115,8 +116,8 @@
     prev_hbm, cur_hbm, pot_hbm, proj_hbm, coup, pattern, counts, pan_hbm,
     out_hbm, coef_out,
     cur, turned, y_low, y_high, z_low, z_high, filt, prev, pot, proj, proj_split,
-    gathered, pan_split, block, repeat, spread_ref, sums, small_a, small_b, near_a, near_b, far_a, far_b,
-    load_sem, halo_send, halo_recv, right_send, left_recv, left_send, right_recv,
+    gathered, pan_split, block, repeat, spread_ref, sums, small_a, small_b, near_a, near_b, far_a, far_b, held,
+    load_sem, halo_send, halo_recv, rest_send, rest_recv, right_send, left_recv, left_send, right_recv,
     sib_send, sib_recv, ahead_send, behind_recv, back_send, front_recv,
     sum_send, sum_recv, store_sem,
 ):
@@ -158,6 +159,10 @@
     partners += [at_z((z + r) % 8) for r in range(1, 8)]
     partners += [up_y, down_y, up_z, down_z]
     partners += [at_band(right), at_band(left), at_band(sibling)]
+    over = (1 - z_hi) * 8
+    after_wrap = {"gy": over + (8 - y) % 8, "gz": gz, "band": band}
+    before_wrap = {"gy": over + (14 - y) % 8, "gz": gz, "band": band}
+    partners += [after_wrap, before_wrap]
     for partner in partners:
         pl.semaphore_signal(barrier, inc=1, device_id=partner, device_id_type=MESH)
     pl.semaphore_wait(barrier, len(partners))
@@ -199,8 +204,26 @@
         pass_on(to_sibling(own_at, k))
 
     load_cur.wait()
-    halo_y0 = remote(cur.at[:, pl.ds(16, 48)], y_low, halo_send.at[0], halo_recv.at[0], up_y)
-    halo_y1 = remote(cur.at[:, pl.ds(0, 48)], y_high, halo_send.at[1], halo_recv.at[1], down_y)
+    first, rest = pl.ds(0, DIRECT), pl.ds(DIRECT, N - DIRECT)
+    upper, lower = pl.ds(16, 48), pl.ds(0, 48)
+    halo_y0 = remote(cur.at[first, upper], y_low.at[first], halo_send.at[0], halo_recv.at[0], up_y)
+    halo_y1 = remote(cur.at[first, lower], y_high.at[first], halo_send.at[1], halo_recv.at[1], down_y)
+    rest_y0 = remote(cur.at[rest, upper], y_low.at[rest], rest_send.at[0], rest_recv.at[0], up_y)
+    rest_y1 = remote(cur.at[rest, lower], y_high.at[rest], rest_send.at[1], rest_recv.at[1], down_y)
+    around_y0 = remote(cur.at[rest, upper], held, rest_send.at[0], rest_recv.at[2], after_wrap)
+    around_y1 = remote(cur.at[rest, lower], held, rest_send.at[1], rest_recv.at[2], before_wrap)
+    onward_y0 = remote(held, y_low.at[rest], rest_send.at[2], rest_recv.at[0], down_y)
+    onward_y1 = remote(held, y_high.at[rest], rest_send.at[2], rest_recv.at[1], up_y)
+
+    def under(condition, action):
+        @pl.when(condition)
+        def _():
+            action()
+
+    under(y == 7, around_y0.start)
+    under(y == 0, around_y1.start)
+    under(y != 7, rest_y0.start)
+    under(y != 0, rest_y1.start)
     halo_y0.start()
     halo_y1.start()
 
@@ -298,6 +321,16 @@
             pass_on(to_left(right_at, opposite_at, k, back_send, front_recv, k - 2))
         pass_on(to_sibling(right_at, k))
 
+    @pl.when(y == 1)
+    def _():
+        around_y0.wait_recv()
+        onward_y0.start()
+
+    @pl.when(y == 6)
+    def _():
+        around_y1.wait_recv()
+        onward_y1.start()
+
     def take(slot):
         for k in range(4):
             to_sibling(slot, k).wait_recv()
@@ -322,8 +355,8 @@
     take(left_at)
     convert(gathered, pan_split, (left_at + 1) * SHARD, SHARD)
 
-    halo_y0.wait_recv()
-    halo_y1.wait_recv()
+    for copy in (halo_y0, halo_y1, rest_y0, rest_y1):
+        copy.wait_recv()
 
     def stencil(rows):
         result = []
@@ -344,32 +377,32 @@
         for at in range(C):
             filt[n, at * 8 : at * 8 + 8, :] += parts[at]
 
+    halo_z0.wait_recv()
+    halo_z1.wait_recv()
+
+    @pl.loop(0, N)
+    def _(n):
+        parts = stencil(lines(z_low, n, 6) + lines(turned, n, 8) + lines(z_high, n, 6))
+        for at in range(C):
+            filt[n, pl.ds(at, 8, stride=8), :] += parts[at]
+
+    transpose_block(filt, block)
+
+    contract(pan_split, block, sums, 0, NEAR)
+    near = fold_layers(sums[0:NEAR, :])
+    near_a[y, 0:16, :] = near[:, 0:128]
+    near_a[y, 16:24, :] = pack(near[:, 128:NEAR])
+    sent += send_y(near_a, 2)
     for k in (0, 1):
         to_right(left_at, opposite_at, k, ahead_send, behind_recv, k).wait_recv()
         pass_on(to_sibling(opposite_at, k))
         to_left(right_at, opposite_at, k + 2, back_send, front_recv, k).wait_recv()
         pass_on(to_sibling(opposite_at, k + 2))
-
-    halo_z0.wait_recv()
-    halo_z1.wait_recv()
-
-    @pl.loop(0, N)
-    def _(n):
-        parts = stencil(lines(z_low, n, 6) + lines(turned, n, 8) + lines(z_high, n, 6))
-        for at in range(C):
-            filt[n, pl.ds(at, 8, stride=8), :] += parts[at]
-
-    transpose_block(filt, block)
-
-    contract(pan_split, block, sums, 0, NEAR)
-    near = fold_layers(sums[0:NEAR, :])
-    near_a[y, 0:16, :] = near[:, 0:128]
-    near_a[y, 16:24, :] = pack(near[:, 128:NEAR])
-    sent += send_y(near_a, 2)
     convert(gathered, pan_split, opposite_at * SHARD, SHARD)
+    contract(pan_split, block, sums, NEAR, SHARD)
     take(opposite_at)
     convert(gathered, pan_split, (opposite_at + 1) * SHARD, SHARD)
-    contract(pan_split, block, sums, NEAR, NP - NEAR)
+    contract(pan_split, block, sums, NEAR + SHARD, SHARD)
     far_a[y] = pack(fold_layers(sums[NEAR:NP, :]))
     sent += send_y(far_a, 3)
     receive(near_a, 2, y)
@@ -412,8 +445,9 @@
         stores[-1].start()
     write_coefs(far, opposite_at)
 
-    for copy in started + sent + [halo_y0, halo_y1, halo_z0, halo_z1]:
+    for copy in started + sent + [halo_y0, halo_y1, rest_y0, rest_y1, halo_z0, halo_z1]:
         copy.wait_send()
+    under((y == 1) | (y == 6), onward_y0.wait_send)
     for copy in stores:
         copy.wait()
 
@@ -454,9 +488,12 @@
             vmem((8, 24, 128), F32),
             vmem((8, 8, 128), F32),
             vmem((8, 8, 128), F32),
+            vmem((N - DIRECT, 48, X), F32),
             dma((5,)),
             dma((4,)),
             dma((4,)),
+            dma((3,)),
+            dma((3,)),
             dma((4,)),
             dma((4,)),
             dma((4,)),

time: 76.8 us -> 71.6 us (0.932)
  the two profiles are of different devices: /device:TPU:18 before, /device:TPU:1 now
where the time goes in v3:
time: 71.6 us; the launch traced here: 71.4 us
  Pallas kernels  67.3 us (94%)
  local copies, waits for them, and re-layouts  3.46 us (5%)
    pallas_call x1, Pallas kernels, per_device(): pl.pallas_call(kernel, out_shape=(jax.ShapeDtypeStruct((N, rows, X), F32)...  67.3 us
    unnamed x2, local copies, waits for them, and re-layouts  3.46 us

profile of v3, /device:TPU:1, one launch (start us, length us, event | category | flops | bytes accessed | tf_op | source)
XLA Modules:
  0.0 71.4 jit_solution(18297188069683983038)
XLA Ops:
  0.6 67.3 %filter_step.1 = (f32[16,64,128]{2,1,0:T(8,128)}, f32[256,16]{1,0:T(8,128)}) custom-call(f32[16,64,128]{2,1,0:T(8,128)} %bitcast.9, f32[16,64,128]{2,1,0:T(8,128)} %bitcast.10, f32[64,128]{1,0:T(8,128)} %bitcast.11, f32[64,64,128]{2,1,0:T(8,128)} %bitcast.6, f32[64]{0:T(128)} %coup.1, s32[8,64]{1,0:T(8,128)} %pattern.1, s32[8]{0:T(128)} %counts.1, ...), custom_call_target="tpu_custom_call" | custom-call | flops 1000000000 | bytes 5242880 | tf_op jit(solution)/shard_map/filter_step/pallas_call | solution.py:459
  67.9 1.6 %copy.10 = f32[256,16]{0,1:T(8,128)} copy(f32[256,16]{1,0:T(8,128)} %get-tuple-element.7) | data formatting | bytes 32768
  69.5 1.9 %copy.12 = f32[16,8,8,128]{3,2,1,0:T(8,128)} copy(f32[16,8,8,128]{3,2,1,0:T(8,128)} %bitcast.8) | data formatting | bytes 1048576

commit v4 on v3

--- a/solution.py
+++ b/solution.py
@@ -26,6 +26,7 @@
 NP = 256
 NEAR = 192
 CHUNK = 8
+PIECE = 4
 DIRECT = 8
 F32 = jnp.float32
 BF16 = jnp.bfloat16
@@ -116,7 +117,7 @@
     prev_hbm, cur_hbm, pot_hbm, proj_hbm, coup, pattern, counts, pan_hbm,
     out_hbm, coef_out,
     cur, turned, y_low, y_high, z_low, z_high, filt, prev, pot, proj, proj_split,
-    gathered, pan_split, block, repeat, spread_ref, sums, small_a, small_b, near_a, near_b, far_a, far_b, held,
+    gathered, pan_split, block, repeat, spread_ref, sums, small_a, small_b, near_a, near_b, far_a, far_b, held, coef_rows,
     load_sem, halo_send, halo_recv, rest_send, rest_recv, right_send, left_recv, left_send, right_recv,
     sib_send, sib_recv, ahead_send, behind_recv, back_send, front_recv,
     sum_send, sum_recv, store_sem,
@@ -173,20 +174,20 @@
             device_id=device, device_id_type=MESH,
         )
 
-    def panel_copy(slot, there, k, send, recv, device):
-        source = gathered.at[pl.ds(slot * SHARD + k * CHUNK, CHUNK)]
-        target = gathered.at[pl.ds(there * SHARD + k * CHUNK, CHUNK)]
+    def panel_copy(slot, there, k, size, send, recv, device):
+        source = gathered.at[pl.ds(slot * SHARD + k * size, size)]
+        target = gathered.at[pl.ds(there * SHARD + k * size, size)]
         return remote(source, target, send, recv, device)
 
-    def to_right(slot, there, k, sems, recvs, at):
-        return panel_copy(slot, there, k, sems.at[at], recvs.at[at], at_band(right))
-
-    def to_left(slot, there, k, sems, recvs, at):
-        return panel_copy(slot, there, k, sems.at[at], recvs.at[at], at_band(left))
-
-    def to_sibling(slot, k):
+    def to_right(slot, there, k, sems, recvs, at, size=CHUNK):
+        return panel_copy(slot, there, k, size, sems.at[at], recvs.at[at], at_band(right))
+
+    def to_left(slot, there, k, sems, recvs, at, size=CHUNK):
+        return panel_copy(slot, there, k, size, sems.at[at], recvs.at[at], at_band(left))
+
+    def to_sibling(slot, k, size=CHUNK):
         at = slot // 2 * 4 + k
-        return panel_copy(slot, slot + 1, k, sib_send.at[at], sib_recv.at[at], at_band(sibling))
+        return panel_copy(slot, slot + 1, k, size, sib_send.at[at], sib_recv.at[at], at_band(sibling))
 
     load_pan.wait()
     started = []
@@ -313,12 +314,14 @@
         k = step
         to_right(own_at, left_at, k, right_send, left_recv, k).wait_recv()
         if k < 2:
-            pass_on(to_right(left_at, opposite_at, k, ahead_send, behind_recv, k))
+            for i in (2 * k, 2 * k + 1):
+                pass_on(to_right(left_at, opposite_at, i, ahead_send, behind_recv, i, PIECE))
         pass_on(to_sibling(left_at, k))
         k = (step + 2) % 4
         to_left(own_at, right_at, k, left_send, right_recv, k).wait_recv()
         if k >= 2:
-            pass_on(to_left(right_at, opposite_at, k, back_send, front_recv, k - 2))
+            for i in (2 * k, 2 * k + 1):
+                pass_on(to_left(right_at, opposite_at, i, back_send, front_recv, i - 4, PIECE))
         pass_on(to_sibling(right_at, k))
 
     @pl.when(y == 1)
@@ -393,14 +396,15 @@
     near_a[y, 0:16, :] = near[:, 0:128]
     near_a[y, 16:24, :] = pack(near[:, 128:NEAR])
     sent += send_y(near_a, 2)
-    for k in (0, 1):
-        to_right(left_at, opposite_at, k, ahead_send, behind_recv, k).wait_recv()
-        pass_on(to_sibling(opposite_at, k))
-        to_left(right_at, opposite_at, k + 2, back_send, front_recv, k).wait_recv()
-        pass_on(to_sibling(opposite_at, k + 2))
+    for i in range(4):
+        to_right(left_at, opposite_at, i, ahead_send, behind_recv, i, PIECE).wait_recv()
+        pass_on(to_sibling(opposite_at, i, PIECE))
+        to_left(right_at, opposite_at, i + 4, back_send, front_recv, i, PIECE).wait_recv()
+        pass_on(to_sibling(opposite_at, i + 4, PIECE))
     convert(gathered, pan_split, opposite_at * SHARD, SHARD)
     contract(pan_split, block, sums, NEAR, SHARD)
-    take(opposite_at)
+    for i in range(8):
+        to_sibling(opposite_at, i, PIECE).wait_recv()
     convert(gathered, pan_split, (opposite_at + 1) * SHARD, SHARD)
     contract(pan_split, block, sums, NEAR + SHARD, SHARD)
     far_a[y] = pack(fold_layers(sums[NEAR:NP, :]))
@@ -425,7 +429,7 @@
         values = coefs.T
         for i in range(coefs.shape[1] // SHARD):
             rows = pl.ds(pl.multiple_of(owners[slot + i] * SHARD, SHARD), SHARD)
-            coef_out[rows, :] = values[i * SHARD : (i + 1) * SHARD, :]
+            coef_rows[rows, :] = values[i * SHARD : (i + 1) * SHARD, :]
 
     receive(near_b, 4, z)
     packed = total(near_b)
@@ -444,12 +448,18 @@
         stores.append(pltpu.make_async_copy(filt.at[:, rows], out_hbm.at[:, rows], store_sem.at[part]))
         stores[-1].start()
     write_coefs(far, opposite_at)
+    coef_out[...] = coef_rows[...].T
 
     for copy in started + sent + [halo_y0, halo_y1, rest_y0, rest_y1, halo_z0, halo_z1]:
         copy.wait_send()
     under((y == 1) | (y == 6), onward_y0.wait_send)
     for copy in stores:
         copy.wait()
+
+
+def finish(rotated, coefs, rotated_out, coefs_out):
+    rotated_out[...] = rotated[...]
+    coefs_out[...] = coefs[...]
 
 
 def per_device(previous, current, potential, projectors, couplings, pattern, counts, panels):
@@ -460,7 +470,7 @@
         kernel,
         out_shape=(
             jax.ShapeDtypeStruct((N, rows, X), F32),
-            jax.ShapeDtypeStruct((NP, N), F32),
+            jax.ShapeDtypeStruct((N, NP), F32),
         ),
         in_specs=[ANY, ANY, ANY, ANY, SMEM, SMEM, SMEM, ANY],
         out_specs=(ANY, pl.BlockSpec(memory_space=pltpu.VMEM)),
@@ -489,6 +499,7 @@
             vmem((8, 8, 128), F32),
             vmem((8, 8, 128), F32),
             vmem((N - DIRECT, 48, X), F32),
+            vmem((NP, N), F32),
             dma((5,)),
             dma((4,)),
             dma((4,)),
@@ -498,12 +509,12 @@
             dma((4,)),
             dma((4,)),
             dma((4,)),
-            dma((16,)),
-            dma((16,)),
-            dma((2,)),
-            dma((2,)),
-            dma((2,)),
-            dma((2,)),
+            dma((20,)),
+            dma((20,)),
+            dma((4,)),
+            dma((4,)),
+            dma((4,)),
+            dma((4,)),
             dma((6, 8)),
             dma((6, 8)),
             dma((4,)),
@@ -523,7 +534,17 @@
         counts,
         panels.reshape(SHARD, rows, X),
     )
-    return rotated.reshape(N, C, C, X), coefs
+    rotated, coefs = pl.pallas_call(
+        finish,
+        out_shape=(
+            jax.ShapeDtypeStruct((N, rows, X), F32),
+            jax.ShapeDtypeStruct((N, NP), F32),
+        ),
+        in_specs=[pl.BlockSpec(memory_space=pltpu.VMEM), pl.BlockSpec(memory_space=pltpu.VMEM)],
+        out_specs=(pl.BlockSpec(memory_space=pltpu.VMEM), pl.BlockSpec(memory_space=pltpu.VMEM)),
+        name="finish",
+    )(rotated, coefs)
+    return rotated.reshape(N, C, C, X), coefs.T
 
 
 def solution(mesh):

time: 71.6 us -> 69.8 us (0.975)
  local copies, waits for them, and re-layouts: 3.46 us -> 0 us
  Pallas kernels: 67.3 us -> 69 us
    unnamed x2 -> x0, local copies, waits for them, and re-layouts: 3.46 us -> none
    pallas_call x0 -> x1, Pallas kernels: none -> 1.87 us  [per_device(): pl.pallas_call(finish, out_shape=(jax.ShapeDtypeStruct((N, rows, X), F32)...]
where the time goes in v4:
time: 69.8 us; the launch traced here: 69.7 us
  Pallas kernels  69 us (99%)
    pallas_call x1, Pallas kernels, per_device(): pl.pallas_call(kernel, out_shape=(jax.ShapeDtypeStruct((N, rows, X), F32)...  67.2 us
    pallas_call x1, Pallas kernels, per_device(): pl.pallas_call(finish, out_shape=(jax.ShapeDtypeStruct((N, rows, X), F32)...  1.87 us

profile of v4, /device:TPU:1, one launch (start us, length us, event | category | flops | bytes accessed | tf_op | source)
XLA Modules:
  0.0 69.7 jit_solution(12800886577493131752)
XLA Ops:
  0.6 67.2 %filter_step.1 = (f32[16,64,128]{2,1,0:T(8,128)}, f32[16,256]{1,0:T(8,128)}) custom-call(f32[16,64,128]{2,1,0:T(8,128)} %bitcast.9, f32[16,64,128]{2,1,0:T(8,128)} %bitcast.10, f32[64,128]{1,0:T(8,128)} %bitcast.11, f32[64,64,128]{2,1,0:T(8,128)} %bitcast.7, f32[64]{0:T(128)} %coup.1, s32[8,64]{1,0:T(8,128)} %pattern.1, s32[8]{0:T(128)} %counts.1, ...), custom_call_target="tpu_custom_call" | custom-call | flops 1000000000 | bytes 5242880 | tf_op jit(solution)/shard_map/filter_step/pallas_call | solution.py:469
  67.8 1.9 %finish.1 = (f32[16,64,128]{2,1,0:T(8,128)}, f32[16,256]{1,0:T(8,128)}) custom-call(f32[16,64,128]{2,1,0:T(8,128)} %get-tuple-element.6.rotated, f32[16,256]{1,0:T(8,128)} %get-tuple-element.7.coefs), custom_call_target="tpu_custom_call" | custom-call | tf_op jit(solution)/shard_map/finish/pallas_call | solution.py:537

commit v5 on v4

--- a/solution.py
+++ b/solution.py
@@ -27,7 +27,9 @@
 NEAR = 192
 CHUNK = 8
 PIECE = 4
-DIRECT = 8
+DIRECT = 6
+ROUND = 5
+FAR_FIRST = (4, 3, 5, 2, 6, 1, 7)
 F32 = jnp.float32
 BF16 = jnp.bfloat16
 MESH = pl.DeviceIdType.MESH
@@ -70,7 +72,7 @@
         target[y * X : (y + 1) * X, 128:256] = low
 
 
-def contract(table, block, sums, first, count):
+def contract(table, block, sums, first, count, shift=0):
     @pl.loop(0, count // 32)
     def _(step):
         start = pl.multiple_of(first + step * 32, 32)
@@ -78,7 +80,7 @@
         full = dot(table[rows, 0:1024], block[...]) + dot(table[rows, 1024:2048], block[...])
         both = full[:, 0:128] + full[:, 128:256]
         kept = jnp.where(same_layer(256, 128), both, 0.0)
-        sums[pl.ds(start, 32), :] = kept.reshape(32, 8, 128).sum(axis=1)
+        sums[pl.ds(start + shift, 32), :] = kept.reshape(32, 8, 128).sum(axis=1)
 
 
 def fold_layers(sums):
@@ -117,10 +119,10 @@
     prev_hbm, cur_hbm, pot_hbm, proj_hbm, coup, pattern, counts, pan_hbm,
     out_hbm, coef_out,
     cur, turned, y_low, y_high, z_low, z_high, filt, prev, pot, proj, proj_split,
-    gathered, pan_split, block, repeat, spread_ref, sums, small_a, small_b, near_a, near_b, far_a, far_b, held, coef_rows,
+    gathered, pan_split, block, repeat, spread_ref, sums, small_a, small_b, near_a, near_b, far_a, far_b, held, coef_rows, far_c, other_filt, other_block,
     load_sem, halo_send, halo_recv, rest_send, rest_recv, right_send, left_recv, left_send, right_recv,
     sib_send, sib_recv, ahead_send, behind_recv, back_send, front_recv,
-    sum_send, sum_recv, store_sem,
+    sum_send, sum_recv, store_sem, mirror_sem,
 ):
     gy, gz, band = lax.axis_index("gy"), lax.axis_index("gz"), lax.axis_index("band")
     z_hi, y = gy // 8, gy % 8
@@ -142,6 +144,9 @@
     down_z = {"gy": gy, "gz": (gz + 3) % 4, "band": band}
     right, left = ((x + 1) % 4) * 2 + core, ((x + 3) % 4) * 2 + core
     opposite, sibling = ((x + 2) % 4) * 2 + core, x * 2 + 1 - core
+
+    def at_other_core(other):
+        return {"gy": (other // 4) * 8 + y, "gz": other % 4, "band": sibling}
 
     own_at, right_at, left_at, opposite_at = 0, 2, 4, 6
     owners = [band, sibling]
@@ -156,14 +161,17 @@
         load.start()
 
     barrier = pltpu.get_barrier_semaphore()
-    partners = [at_y((y + r) % 8) for r in range(1, 8)]
-    partners += [at_z((z + r) % 8) for r in range(1, 8)]
-    partners += [up_y, down_y, up_z, down_z]
+    partners = [at_y((y + r) % 8) for r in FAR_FIRST]
+    partners += [at_z((z + r) % 8) for r in FAR_FIRST]
     partners += [at_band(right), at_band(left), at_band(sibling)]
+    partners += [at_other_core((z + r) % 8) for r in FAR_FIRST]
     over = (1 - z_hi) * 8
     after_wrap = {"gy": over + (8 - y) % 8, "gz": gz, "band": band}
     before_wrap = {"gy": over + (14 - y) % 8, "gz": gz, "band": band}
-    partners += [after_wrap, before_wrap]
+    across = {"gy": over + 7 - y, "gz": gz, "band": band}
+    after_next = {"gy": over + (9 - y) % 8, "gz": gz, "band": band}
+    before_next = {"gy": over + (13 - y) % 8, "gz": gz, "band": band}
+    partners = [after_wrap, before_wrap, after_next, before_next, across] + partners
     for partner in partners:
         pl.semaphore_signal(barrier, inc=1, device_id=partner, device_id_type=MESH)
     pl.semaphore_wait(barrier, len(partners))
@@ -196,35 +204,42 @@
         copy.start()
         started.append(copy)
 
-    for step in range(4):
-        k = step
-        pass_on(to_right(own_at, left_at, k, right_send, left_recv, k))
-        k = (step + 2) % 4
-        pass_on(to_left(own_at, right_at, k, left_send, right_recv, k))
+    def send_own(steps):
+        for step in steps:
+            pass_on(to_right(own_at, left_at, step, right_send, left_recv, step))
+            k = (step + 2) % 4
+            pass_on(to_left(own_at, right_at, k, left_send, right_recv, k))
+
+    send_own((0, 1))
     for k in range(4):
         pass_on(to_sibling(own_at, k))
 
     load_cur.wait()
-    first, rest = pl.ds(0, DIRECT), pl.ds(DIRECT, N - DIRECT)
+    first = pl.ds(0, DIRECT)
     upper, lower = pl.ds(16, 48), pl.ds(0, 48)
     halo_y0 = remote(cur.at[first, upper], y_low.at[first], halo_send.at[0], halo_recv.at[0], up_y)
     halo_y1 = remote(cur.at[first, lower], y_high.at[first], halo_send.at[1], halo_recv.at[1], down_y)
-    rest_y0 = remote(cur.at[rest, upper], y_low.at[rest], rest_send.at[0], rest_recv.at[0], up_y)
-    rest_y1 = remote(cur.at[rest, lower], y_high.at[rest], rest_send.at[1], rest_recv.at[1], down_y)
-    around_y0 = remote(cur.at[rest, upper], held, rest_send.at[0], rest_recv.at[2], after_wrap)
-    around_y1 = remote(cur.at[rest, lower], held, rest_send.at[1], rest_recv.at[2], before_wrap)
-    onward_y0 = remote(held, y_low.at[rest], rest_send.at[2], rest_recv.at[0], down_y)
-    onward_y1 = remote(held, y_high.at[rest], rest_send.at[2], rest_recv.at[1], up_y)
 
     def under(condition, action):
         @pl.when(condition)
         def _():
             action()
 
-    under(y == 7, around_y0.start)
-    under(y == 0, around_y1.start)
-    under(y != 7, rest_y0.start)
-    under(y != 0, rest_y1.start)
+    plain, around, onward = [], [], []
+    for i, (after, before) in enumerate(((after_wrap, before_wrap), (after_next, before_next))):
+        rest = pl.ds(DIRECT + i * ROUND, ROUND)
+        s0, s1, s2 = (rest_send.at[k * 2 + i] for k in range(3))
+        r0, r1, r2 = (rest_recv.at[k * 2 + i] for k in range(3))
+        plain.append(remote(cur.at[rest, upper], y_low.at[rest], s0, r0, up_y))
+        plain.append(remote(cur.at[rest, lower], y_high.at[rest], s1, r1, down_y))
+        around.append(remote(cur.at[rest, upper], held, s0, r2, after))
+        around.append(remote(cur.at[rest, lower], held, s1, r2, before))
+        onward.append(remote(held, y_low.at[rest], s2, r0, at_y(0)))
+        onward.append(remote(held, y_high.at[rest], s2, r1, at_y(7)))
+    for i in range(4):
+        edge = 7 if i % 2 == 0 else 0
+        under(y == edge, around[i].start)
+        under(y != edge, plain[i].start)
     halo_y0.start()
     halo_y1.start()
 
@@ -256,7 +271,7 @@
 
     def send_y(buffer, sems):
         copies = []
-        for r in range(1, 8):
+        for r in FAR_FIRST:
             copies.append(
                 remote(buffer.at[y], buffer.at[y], sum_send.at[sems, r], sum_recv.at[sems, y], at_y((y + r) % 8))
             )
@@ -265,7 +280,7 @@
 
     def send_z(buffer, sems):
         copies = []
-        for r in range(1, 8):
+        for r in FAR_FIRST:
             copies.append(
                 remote(buffer.at[z], buffer.at[z], sum_send.at[sems, r], sum_recv.at[sems, z], at_z((z + r) % 8))
             )
@@ -296,6 +311,8 @@
         for reach in range(1, 7):
             lap = lap + STENCIL[reach] * (pltpu.roll(value, reach, 1) + pltpu.roll(value, X - reach, 1))
         filt[n] = SCALE * (-0.5 * lap + pot[...] * value - CENTER * value) - prev[n]
+
+    send_own((2, 3))
 
     receive(small_a, 0, y)
     small_b[z] = total(small_a)
@@ -324,15 +341,13 @@
                 pass_on(to_left(right_at, opposite_at, i, back_send, front_recv, i - 4, PIECE))
         pass_on(to_sibling(right_at, k))
 
-    @pl.when(y == 1)
-    def _():
-        around_y0.wait_recv()
-        onward_y0.start()
-
-    @pl.when(y == 6)
-    def _():
-        around_y1.wait_recv()
-        onward_y1.start()
+    def hand_on(i):
+        around[i].wait_recv()
+        onward[i].start()
+
+    holders = (1, 6, 2, 5)
+    for i in range(4):
+        under(y == holders[i], lambda i=i: hand_on(i))
 
     def take(slot):
         for k in range(4):
@@ -353,12 +368,7 @@
             rows = pl.ds((part * 2 + half) * 8, 8)
             filt[:, rows, :] += SCALE * value[:, half * X : (half + 1) * X].reshape(N, 8, X)
 
-    take(right_at)
-    convert(gathered, pan_split, (right_at + 1) * SHARD, SHARD)
-    take(left_at)
-    convert(gathered, pan_split, (left_at + 1) * SHARD, SHARD)
-
-    for copy in (halo_y0, halo_y1, rest_y0, rest_y1):
+    for copy in [halo_y0, halo_y1] + plain:
         copy.wait_recv()
 
     def stencil(rows):
@@ -389,13 +399,23 @@
         for at in range(C):
             filt[n, pl.ds(at, 8, stride=8), :] += parts[at]
 
+    mirror = remote(filt, other_filt, mirror_sem.at[0], mirror_sem.at[1], at_band(sibling))
+    mirror.start()
     transpose_block(filt, block)
 
-    contract(pan_split, block, sums, 0, NEAR)
+    contract(pan_split, block, sums, 0, (right_at + 1) * SHARD)
+    contract(pan_split, block, sums, left_at * SHARD, SHARD)
+    for slot in (right_at, left_at):
+        take(slot)
+        convert(gathered, pan_split, (slot + 1) * SHARD, SHARD)
+        contract(pan_split, block, sums, (slot + 1) * SHARD, SHARD)
     near = fold_layers(sums[0:NEAR, :])
     near_a[y, 0:16, :] = near[:, 0:128]
     near_a[y, 16:24, :] = pack(near[:, 128:NEAR])
     sent += send_y(near_a, 2)
+    mirror.wait_recv()
+    transpose_block(other_filt, other_block)
+
     for i in range(4):
         to_right(left_at, opposite_at, i, ahead_send, behind_recv, i, PIECE).wait_recv()
         pass_on(to_sibling(opposite_at, i, PIECE))
@@ -403,18 +423,22 @@
         pass_on(to_sibling(opposite_at, i + 4, PIECE))
     convert(gathered, pan_split, opposite_at * SHARD, SHARD)
     contract(pan_split, block, sums, NEAR, SHARD)
-    for i in range(8):
-        to_sibling(opposite_at, i, PIECE).wait_recv()
-    convert(gathered, pan_split, (opposite_at + 1) * SHARD, SHARD)
-    contract(pan_split, block, sums, NEAR + SHARD, SHARD)
+    contract(pan_split, other_block, sums, NEAR, SHARD, SHARD)
     far_a[y] = pack(fold_layers(sums[NEAR:NP, :]))
     sent += send_y(far_a, 3)
     receive(near_a, 2, y)
     near_b[z] = total(near_a)
     sent += send_z(near_b, 4)
+    for i in range(8):
+        to_sibling(opposite_at, i, PIECE).wait_recv()
+    convert(gathered, pan_split, (opposite_at + 1) * SHARD, SHARD)
     receive(far_a, 3, y)
     far_b[z] = total(far_a)
     sent += send_z(far_b, 5)
+    for r in (4, 3, 5, 2, 6, 1, 7, 0):
+        other = at_other_core((z + r) % 8)
+        sent.append(remote(far_b.at[z], far_c.at[z], sum_send.at[6, r], sum_recv.at[6, z], other))
+        sent[-1].start()
 
     def take_away(first, count, part):
         at = part * 256
@@ -435,11 +459,17 @@
     packed = total(near_b)
     near = jnp.concatenate([packed[0:16], unpack(packed[16:24])], axis=1)
     spread(near, repeat, spread_ref, 0)
+    mirror.wait_send()
     for part in range(4):
         take_away(0, NEAR, part)
     write_coefs(near, 0)
     receive(far_b, 5, z)
-    far = unpack(total(far_b))
+    for r in range(8):
+        other = (z + r) % 8
+        remote(
+            far_c.at[other], far_c.at[other], sum_send.at[6, r], sum_recv.at[6, other], at_band(sibling)
+        ).wait_recv()
+    far = jnp.concatenate([unpack(total(far_b))[:, 0:SHARD], unpack(total(far_c))[:, SHARD : 2 * SHARD]], axis=1)
     spread(far, repeat, spread_ref, NEAR * 8)
     stores = []
     for part in range(4):
@@ -450,9 +480,10 @@
     write_coefs(far, opposite_at)
     coef_out[...] = coef_rows[...].T
 
-    for copy in started + sent + [halo_y0, halo_y1, rest_y0, rest_y1, halo_z0, halo_z1]:
+    for copy in started + sent + [halo_y0, halo_y1, halo_z0, halo_z1] + plain:
         copy.wait_send()
-    under((y == 1) | (y == 6), onward_y0.wait_send)
+    for i in range(4):
+        under(y == holders[i], onward[i].wait_send)
     for copy in stores:
         copy.wait()
 
@@ -498,13 +529,16 @@
             vmem((8, 24, 128), F32),
             vmem((8, 8, 128), F32),
             vmem((8, 8, 128), F32),
-            vmem((N - DIRECT, 48, X), F32),
+            vmem((ROUND, 48, X), F32),
             vmem((NP, N), F32),
+            vmem((8, 8, 128), F32),
+            vmem((N, rows, X), F32),
+            vmem((1024, 256), BF16),
             dma((5,)),
             dma((4,)),
             dma((4,)),
-            dma((3,)),
-            dma((3,)),
+            dma((6,)),
+            dma((6,)),
             dma((4,)),
             dma((4,)),
             dma((4,)),
@@ -515,9 +549,10 @@
             dma((4,)),
             dma((4,)),
             dma((4,)),
-            dma((6, 8)),
-            dma((6, 8)),
-            dma((4,)),
+            dma((7, 8)),
+            dma((7, 8)),
+            dma((4,)),
+            dma((2,)),
         ],
         compiler_params=pltpu.CompilerParams(
             collective_id=0, has_side_effects=True, vmem_limit_bytes=56 * 1024 * 1024

time: 69.8 us -> 69.8 us (level)
  no operation moved by 1% of the time
where the time goes in v5:
time: 69.8 us; the launch traced here: 69.6 us
  Pallas kernels  69 us (99%)
    pallas_call x1, Pallas kernels, per_device(): pl.pallas_call(kernel, out_shape=(jax.ShapeDtypeStruct((N, rows, X), F32)...  67.1 us
    pallas_call x1, Pallas kernels, per_device(): pl.pallas_call(finish, out_shape=(jax.ShapeDtypeStruct((N, rows, X), F32)...  1.87 us

profile of v5, /device:TPU:1, one launch (start us, length us, event | category | flops | bytes accessed | tf_op | source)
XLA Modules:
  0.0 69.6 jit_solution(10010390453744380350)
XLA Ops:
  0.6 67.1 %filter_step.1 = (f32[16,64,128]{2,1,0:T(8,128)}, f32[16,256]{1,0:T(8,128)}) custom-call(f32[16,64,128]{2,1,0:T(8,128)} %bitcast.9, f32[16,64,128]{2,1,0:T(8,128)} %bitcast.10, f32[64,128]{1,0:T(8,128)} %bitcast.11, f32[64,64,128]{2,1,0:T(8,128)} %bitcast.7, f32[64]{0:T(128)} %coup.1, s32[8,64]{1,0:T(8,128)} %pattern.1, s32[8]{0:T(128)} %counts.1, ...), custom_call_target="tpu_custom_call" | custom-call | flops 1000000000 | bytes 5242880 | tf_op jit(solution)/shard_map/filter_step/pallas_call | solution.py:500
  67.8 1.9 %finish.1 = (f32[16,64,128]{2,1,0:T(8,128)}, f32[16,256]{1,0:T(8,128)}) custom-call(f32[16,64,128]{2,1,0:T(8,128)} %get-tuple-element.6.rotated, f32[16,256]{1,0:T(8,128)} %get-tuple-element.7.coefs), custom_call_target="tpu_custom_call" | custom-call | tf_op jit(solution)/shard_map/finish/pallas_call | solution.py:572
